TPU v7x, 512 devices: a whole 4x8x8 slice. The times are simulated.
512 devices in a mesh: fsdp: 128 (over y_lo, x, z, core), tp: 4 (over y_hi).
Axes of the slice: x: 4, y: 8 (y_hi: 4, y_lo: 2; y = y_hi * 2 + y_lo), z: 8, core: 2. Of those that a mesh axis runs over, the one named last changes fastest.
Arguments:
- token_grads: float32 [32768, 128], P('fsdp'), may hold values from -96 to 96
- hidden: bfloat16 [32768, 2048], P('fsdp', 'tp')
- proj_weight: float32 [128, 2048], P(None, 'tp'), may hold values from -0.125 to 0.125
- proj_bias: float32 [128], replicated, may hold values from -4 to 4
- norm_gain: float32 [2048], P('tp'), may hold values from 0.1 to 1.9
- down_weight: float32 [5632, 2048], P('tp', 'fsdp'), may hold values from -0.5 to 0.5
- lengths: int32 [64], replicated, may hold values from 1 to 512, as said below
Outputs:
- act_grad: bfloat16 [32768, 5632], P('fsdp', 'tp')
- proj_grad: float32 [128, 2048], P(None, 'tp')
- gain_grad: float32 [2048], P('tp')
- bias_grad: float32 [128], replicated
Inputs may be any that keep to these rules, and one draw needn't show every extreme that they name: `lengths`: every sequence has at least one valid token, and some sequence is full.
All inputs are finite; a program needn't handle non-finite values.
Results may differ from a plain program's by a relative error of at most 0.018.
Values may be sent and summed in bfloat16 or wider, within the bound.
A program may use at most 64 MiB of HBM per device.

v0:
```python
import jax
import jax.numpy as jnp
from jax import lax
from jax.sharding import PartitionSpec as P

D = 2048
LEN = 512


def embed_grad(grads, u_proj, inv, proj_bias):
    zvals = inv[:, None] * u_proj + proj_bias
    kinv = lax.rsqrt(jnp.sum(zvals * zvals, axis=1) + 1e-06)
    emb = zvals * kinv[:, None]
    return kinv[:, None] * (grads - emb * jnp.sum(emb * grads, axis=1)[:, None])


def shards(token_grads, hidden, proj_weight, proj_bias, norm_gain, down_weight, lengths):
    high = lax.Precision.HIGHEST
    tok_count = hidden.shape[0]
    emb_width = token_grads.shape[1]
    fsdp_count = lax.axis_size("fsdp")
    piece_rows = tok_count // fsdp_count
    shaped = token_grads.reshape(fsdp_count, piece_rows, emb_width)
    arrived = (
        lax.all_to_all(shaped.astype(jnp.bfloat16), "fsdp", split_axis=0, concat_axis=0, tiled=True)
        .astype(shaped.dtype)
        .reshape(tok_count, emb_width)
    )
    position = lax.axis_index("fsdp") * tok_count + jnp.arange(tok_count, dtype=jnp.int32)
    seq_ids = position // LEN
    seq_table = jnp.arange(lengths.shape[0], dtype=jnp.int32)
    own_length = jnp.sum(
        jnp.where(seq_ids[:, None] == seq_table[None, :], lengths[None, :], 0), axis=1
    )
    grads = jnp.where((position % LEN < own_length)[:, None], arrived, jnp.float32(0.0))
    xvals = hidden.astype(jnp.float32)
    scaled = xvals * norm_gain
    part_u = jnp.dot(scaled, proj_weight.T, precision=high)
    part_sq = jnp.sum(xvals * xvals, axis=1)
    u_proj, sq_sum = (
        lax.psum(part_u.astype(jnp.bfloat16), "tp").astype(jnp.float32),
        lax.psum(part_sq.astype(jnp.bfloat16), "tp").astype(jnp.float32),
    )
    inv = lax.rsqrt(sq_sum / D + 1e-06)
    dz = embed_grad(grads, u_proj, inv, proj_bias)
    dn = jnp.dot(dz, proj_weight, precision=high)
    cvals = jnp.sum(dz * u_proj, axis=1)
    dh_local = (inv[:, None] * norm_gain * dn - xvals * (inv**3 * cvals / D)[:, None]).astype(
        jnp.bfloat16
    )
    dh = lax.all_gather(dh_local, "tp", axis=1, tiled=True)
    normed = scaled * inv[:, None]
    proj_part = jnp.dot(dz.T, normed, precision=high)
    gain_part = jnp.sum(dn * xvals * inv[:, None], axis=0)
    bias_part = jnp.sum(dz, axis=0)
    proj_sum, gain_sum, bias_sum = lax.psum((proj_part, gain_part, bias_part), "fsdp")
    seq_count = jnp.float32(tok_count * fsdp_count // LEN)
    down_low = down_weight.astype(jnp.bfloat16)
    contract = (((1,), (1,)), ((), ()))
    full_down = lax.all_gather(down_low, "fsdp", axis=1, tiled=True)
    act = lax.dot_general(dh, full_down, contract, preferred_element_type=jnp.float32)
    return (
        act.astype(jnp.bfloat16),
        proj_sum / seq_count,
        gain_sum / seq_count,
        bias_sum / seq_count,
    )


def solution(mesh):
    placed = (P("fsdp", None), P("fsdp", "tp"), P(None, "tp"), P(), P("tp"), P("tp", "fsdp"), P())
    return jax.shard_map(
        shards,
        mesh=mesh,
        in_specs=placed,
        out_specs=(P("fsdp", "tp"), P(None, "tp"), P("tp"), P()),
        check_vma=False,
    )
```

profile of v0, /device:TPU:1, one launch (start us, length us, event | category | flops | bytes accessed | tf_op | source)
XLA Modules:
  0.0 1304.3 jit_solution(5737623652718908287)
XLA Ops:
  7.2 0.0 copy-start
  7.2 0.0 all-reduce.4.cloned.1.call-start
  7.2 0.9 copy-done
  8.1 2.2 convolution_convert_fusion.1
  10.3 0.0 all-reduce.4.cloned.1.call-update
  10.3 1.5 convert_element_type.36
  11.9 16.6 %all-to-all-start = ((bf16[128,2,128]{2,1,0:T(2,128)(2,1)}), bf16[128,2,128]{2,1,0:T(2,128)(2,1)S(1)}, u32[]{:S(2)}, u32[]{:S(2)}) async-start(bf16[128,2,128]{2,1,0:T(2,128)(2,1)} %bitcast), calls=%async_computation | async-start | bytes 131072 | tf_op jit(solution)/shard_map/all_to_all | solution.py:25
  28.5 0.0 all-reduce.6.cloned.1.call-start
  28.5 1.1 fusion.3
  29.6 10.7 psum.35
  40.4 0.8 select_reduce_fusion
  41.1 28.3 %all-reduce.4.cloned.1.call-done = bf16[256,128]{1,0:T(8,128)(2,1)} async-done(((bf16[256,128]{1,0:T(8,128)(2,1)}), bf16[256,128]{1,0:T(8,128)(2,1)}) %all-reduce.4.cloned.1.call-update) | async-done | bytes 65552 | tf_op jit(solution)/shard_map/psum | solution.py:41
  69.4 1.0 fusion.19
  70.4 0.0 all-to-all-done
  70.4 1.1 fusion.16
  71.5 2.4 fusion.1
  73.9 0.0 all-reduce.6.cloned.1.call-update
  73.9 0.0 all-gather.3.cloned.1.call-start
  74.0 1.1 fusion.25
  75.1 2.5 fusion.7
  77.6 0.0 all-gather.3.cloned.1.call-update
  77.6 0.0 all-gather.5.cloned.1.call-start
  77.7 1.5 convert_element_type.39
  79.2 0.0 all-gather.5.cloned.1.call-update
  79.2 278.2 %all-reduce = (f32[512]{0:T(512)S(1)}, f32[128]{0:T(128)S(1)}) all-reduce(f32[512]{0:T(512)S(1)} %get-tuple-element.8, f32[128]{0:T(128)S(1)} %get-tuple-element.4), channel_id=1, replica_groups=mesh['fsdp'=128,'tp'=4] {'fsdp'}, use_global_device_ids=true, to_apply=%region_9.10 | all-reduce | flops 640 | bytes 5120 | tf_op jit(solution)/shard_map/psum | solution.py:56
  357.4 0.5 broadcast_multiply_fusion.2
  357.9 0.6 broadcast_multiply_fusion.1
  358.5 677.2 %all-reduce.6.cloned.1.call-done = f32[128,512]{1,0:T(8,128)} async-done(((f32[128,512]{1,0:T(8,128)}), f32[128,512]{1,0:T(8,128)}) %all-reduce.6.cloned.1.call-update) | async-done | bytes 262160 | tf_op jit(solution)/shard_map/psum | solution.py:56
  1035.7 1.7 broadcast_multiply_fusion
  1037.3 34.0 %all-gather.3.cloned.1.call-done = bf16[256,2048]{1,0:T(8,128)(2,1)} async-done(((bf16[256,512]{1,0:T(8,128)(2,1)}), bf16[256,2048]{1,0:T(8,128)(2,1)}) %all-gather.3.cloned.1.call-update) | async-done | bytes 1048592 | tf_op jit(solution)/shard_map/all_gather | solution.py:51
  1071.4 220.8 %all-gather.5.cloned.1.call-done = bf16[1408,2048]{0,1:T(8,128)(2,1)} async-done(((bf16[1408,16]{0,1:T(8,128)(2,1)}), bf16[1408,2048]{0,1:T(8,128)(2,1)}) %all-gather.5.cloned.1.call-update) | async-done | bytes 5767184 | tf_op jit(solution)/shard_map/all_gather | solution.py:60
  1292.1 5.6 convolution_convert_fusion
  (5 shorter events, 0.1 us)
Async XLA Ops:
  7.2 1.0 copy-start
  7.2 62.2 %all-reduce.4.cloned.1.call-start = ((), (), s32[]{:S(2)}) async-start(), calls=%async_computation.1 | async-start | bytes 131072 | tf_op jit(solution)/shard_map/psum | solution.py:41
  11.9 58.6 %all-to-all-start = ((bf16[128,2,128]{2,1,0:T(2,128)(2,1)}), bf16[128,2,128]{2,1,0:T(2,128)(2,1)S(1)}, u32[]{:S(2)}, u32[]{:S(2)}) async-start(bf16[128,2,128]{2,1,0:T(2,128)(2,1)} %bitcast), calls=%async_computation | async-start | bytes 131072 | tf_op jit(solution)/shard_map/all_to_all | solution.py:25
  28.5 1007.2 %all-reduce.6.cloned.1.call-start = ((), (), s32[]{:S(2)}) async-start(), calls=%async_computation.4 | async-start | bytes 524288 | tf_op jit(solution)/shard_map/psum | solution.py:56
  73.9 997.4 %all-gather.3.cloned.1.call-start = ((), (), s32[]{:S(2)}) async-start(), calls=%async_computation.2 | async-start | bytes 1310720 | tf_op jit(solution)/shard_map/all_gather | solution.py:51
  77.6 1214.5 %all-gather.5.cloned.1.call-start = ((), (), s32[]{:S(2)}) async-start(), calls=%async_computation.3 | async-start | bytes 5812224 | tf_op jit(solution)/shard_map/all_gather | solution.py:60
Sparse Core Ops, SparseCore 0:
  11.5 57.8 all-reduce.3
  74.0 961.5 all-reduce.5
  1038.4 32.9 all-gather.2
  1073.4 218.7 all-gather.4
where the time goes:
time: 1300 us
  waiting for transfers between devices  960 us (74%)
  blocking collectives  289 us (22%)
  starting transfers between devices  16.8 us (1%)
  between operations  13.8 us (1%)
    psum x1, waiting for transfers between devices, shards(): lax.psum((proj_part, gain_part, bias_part), 'fsdp')  677 us
    psum x1, blocking collectives, shards(): lax.psum((proj_part, gain_part, bias_part), 'fsdp')  278 us
    all_gather x1, waiting for transfers between devices, shards(): full_down = lax.all_gather(down_low, 'fsdp', axis=1, tiled=True)  221 us
    all_gather x1, waiting for transfers between devices, shards(): dh = lax.all_gather(dh_local, 'tp', axis=1, tiled=True)  34 us
    psum x1, waiting for transfers between devices, shards(): lax.psum(part_u.astype(jnp.bfloat16), 'tp').astype(jnp.float32)  28.3 us
  transfers between devices with their start and end apart: 5, of which 4 were waited for; matrix products, arithmetic and copies ran while one was open for 1% of the time, Pallas kernels for 0%

commit v1 on v0

v1 whole, which is shorter than its diff:
```python
import jax
import jax.numpy as jnp
from jax import lax
from jax.experimental import pallas as pl
from jax.experimental.pallas import tpu as pltpu
from jax.sharding import PartitionSpec as P

D = 2048
LEN = 512
NX, NZ, NG, NP, NT = 4, 8, 8, 16, 4
MESH = pl.DeviceIdType.MESH
HIGH = lax.Precision.HIGHEST
BF, F32, I32 = jnp.bfloat16, jnp.float32, jnp.int32
NT_DIMS = (((1,), (1,)), ((), ()))


def iota(shape, axis):
    return lax.broadcasted_iota(I32, shape, axis)


def split_hi_lo(value):
    hi = value.astype(BF).astype(F32)
    return hi, value - hi


def permute_rows(count, source_of, rows):
    hot = jnp.where(
        iota((count, count), 1) == source_of(iota((count, count), 0)), F32(1.0), F32(0.0)
    ).astype(BF)
    return jnp.dot(hot, rows, preferred_element_type=F32)


def kernel(
    tg_ref, x_ref, p_ref, b_ref, g_ref, w_ref, len_ref,
    act_ref, proj_ref, gain_ref, bias_ref,
    wfull, usend, urecv, s1src, s1dst, s2src, s2dst, dzfull, dhfull, rs_src, rs_dst, zbuf, ag,
    a1s, a1r, zs0, zr0, b1s, b1r, zs1, zr1, xs, xr, xfs, xfr, sibs, sibr,
    s1ss, s1rs, s2ss, s2rs, us, ur, ds, dr, dhs, dhr, dfs, dfr, rss, rsr, zss, zsr, ags, agr,
):
    f = lax.axis_index("fsdp")
    t = lax.axis_index("tp")
    core = f % 2
    z = (f // 2) % NZ
    grp = f // 16
    xa = grp % NX
    yl = grp // NX
    p = grp * 2 + core

    def at_f(group, zpos, cpos):
        return group * 16 + zpos * 2 + cpos

    def peer_p(d):
        q = (p + d) % NP
        return q, at_f(q // 2, z, q % 2)

    def peer_z(d):
        q = (z + d) % NZ
        return q, at_f(grp, q, core)

    def peer_t(d):
        return (t + d) % NT

    def copy(src, dst, ssem, rsem, dev):
        return pltpu.make_async_remote_copy(
            src_ref=src, dst_ref=dst, send_sem=ssem, recv_sem=rsem,
            device_id=dev, device_id_type=MESH,
        )

    def each(lo, hi, body):
        def step(d, carry):
            body(d)
            return carry

        lax.fori_loop(lo, hi, step, 0)

    bar = pltpu.get_barrier_semaphore()

    def greet(dev):
        pl.semaphore_signal(bar, inc=1, device_id=dev, device_id_type=MESH)

    each(1, NP, lambda d: greet({"fsdp": peer_p(d)[1]}))
    each(1, NZ, lambda d: greet({"fsdp": peer_z(d)[1]}))
    each(1, NT, lambda d: greet({"tp": peer_t(d)}))

    wfull[yl, xa, z, core] = w_ref[...].astype(BF)
    tg = permute_rows(
        256, lambda r: ((r >> 2) & 7) * 32 + (r >> 5) * 4 + (r & 3), tg_ref[...].astype(BF)
    )
    s1src[...] = tg.astype(BF).reshape(8, 32, 128)
    xv = x_ref[...].astype(F32)
    pu = lax.dot_general(xv * g_ref[...], p_ref[...], NT_DIMS, precision=HIGH)
    sq_hi, sq_lo = split_hi_lo(jnp.sum(xv * xv, axis=1, keepdims=True))
    sq2 = jnp.where(iota((256, 128), 1) < 64, sq_hi, sq_lo)
    usend[:, :, :, 0:128] = pu.astype(BF).reshape(2, 4, 32, 128)
    usend[:, :, :, 128:256] = sq2.astype(BF).reshape(2, 4, 32, 128)
    pl.semaphore_wait(bar, (NP - 1) + (NZ - 1) + (NT - 1))

    sends0, sends1 = [], []

    def go(sends, make):
        make().start()
        sends.append(make)

    def sibling(piece):
        copy(piece, piece, sibs, sibr, {"fsdp": f + 1 - 2 * core}).start()

    own = wfull.at[yl, xa, z, core]
    zdev = ({"fsdp": at_f(grp, (z + 1) % NZ, core)}, {"fsdp": at_f(grp, (z + NZ - 1) % NZ, core)})
    xdev = (
        {"fsdp": at_f(yl * NX + (xa + 1) % NX, z, core)},
        {"fsdp": at_f(yl * NX + (xa + NX - 1) % NX, z, core)},
    )

    def zslot(direction, s):
        return (z + NZ - s) % NZ if direction == 0 else (z + s) % NZ

    def piece0(h, zj):
        return wfull.at[h, :, zj, 0]

    def zmove0(direction, s, h):
        def make():
            piece = piece0(h, zslot(direction, s))
            return copy(piece, piece, zs0.at[direction, s, h], zr0.at[direction, s, h], zdev[direction])

        return make

    def begin0():
        for d in range(1, NG):
            go(sends0, lambda d=d: copy(
                own, own, a1s.at[d], a1r.at[d], {"fsdp": at_f((grp + d) % NG, z, core)}))

    def first0():
        for d in range(1, NG):
            copy(own, own, a1s.at[d], a1r.at[d], zdev[0]).wait_recv()
        for direction, h in ((0, 0), (1, 1), (0, 1), (1, 0)):
            go(sends0, zmove0(direction, 0, h))
        sibling(wfull.at[:, :, z, 0])

    def step0(s, direction, h):
        def run():
            zmove0(direction, s - 1, h)().wait_recv()
            if s < 3 or (s == 3 and h == direction):
                go(sends0, zmove0(direction, s, h))
            sibling(piece0(h, zslot(direction, s)))

        return run

    todo0 = [first0]
    for s in (1, 2, 3):
        todo0 += [step0(s, d, h) for d, h in ((0, 0), (1, 1), (0, 1), (1, 0))]
    todo0 += [step0(4, 0, 0), step0(4, 1, 1)]

    hops = [(0, 0), (0, 1), (1, 1), (0, 2), (1, 2), (0, 3), (1, 3), (0, 4)]

    def piece1(xj, zj):
        return wfull.at[:, xj, zj, 1]

    def zmove1(direction, s):
        def make():
            piece = piece1(xa, zslot(direction, s))
            return copy(piece, piece, zs1.at[direction, s], zr1.at[direction, s], zdev[direction])

        return make

    def xmove(direction, k):
        def make():
            piece = piece1(xa, zslot(*hops[k]))
            return copy(piece, piece, xs.at[direction, k], xr.at[direction, k], xdev[direction])

        return make

    def xforward(k):
        direction = k % 2

        def make():
            xj = (xa + NX - 1) % NX if direction == 0 else (xa + 1) % NX
            piece = piece1(xj, zslot(*hops[k]))
            return copy(piece, piece, xfs.at[k], xfr.at[k], xdev[direction])

        return make

    def begin1():
        go(sends1, lambda: copy(own, own, b1s, b1r, {"fsdp": at_f((grp + NX) % NG, z, core)}))

    def spread(k):
        go(sends1, xmove(0, k))
        go(sends1, xmove(1, k))
        sibling(piece1(xa, zslot(*hops[k])))

    def first1():
        copy(own, own, b1s, b1r, zdev[0]).wait_recv()
        go(sends1, zmove1(0, 0))
        go(sends1, zmove1(1, 0))
        spread(0)

    def zstep1(k):
        def run():
            direction, s = hops[k]
            zmove1(direction, s - 1)().wait_recv()
            if s < 3 or (s == 3 and direction == 0):
                go(sends1, zmove1(direction, s))
            spread(k)

        return run

    def xstep1(k, direction):
        def run():
            xmove(direction, k)().wait_recv()
            xj = (xa + NX - 1) % NX if direction == 0 else (xa + 1) % NX
            if k % 2 == direction:
                go(sends1, xforward(k))
            sibling(piece1(xj, zslot(*hops[k])))

        return run

    def fstep1(k):
        def run():
            xforward(k)().wait_recv()
            sibling(piece1((xa + 2) % NX, zslot(*hops[k])))

        return run

    todo1 = [first1]
    for k in range(1, 8):
        todo1.append(zstep1(k))
        if k >= 3:
            todo1 += [xstep1(k - 3, 0), xstep1(k - 3, 1)]
        if k >= 6:
            todo1.append(fstep1(k - 6))
    for k in (5, 6, 7):
        todo1 += [xstep1(k, 0), xstep1(k, 1), fstep1(k - 3)]
    todo1 += [fstep1(k) for k in (5, 6, 7)]

    def advance(n0, n1):
        head0, head1 = todo0[:n0], todo1[:n1]
        del todo0[:n0], todo1[:n1]
        if head0:
            @pl.when(core == 0)
            def _():
                for run in head0:
                    run()
        if head1:
            @pl.when(core == 1)
            def _():
                for run in head1:
                    run()

    todo0.insert(0, begin0)
    todo1.insert(0, begin1)
    advance(1, 1)

    carries = xa == t

    @pl.when(carries)
    def _():
        def send(d):
            q, dev = peer_z(d)
            copy(s1src.at[q], s1dst.at[z], s1ss.at[d], s1rs.at[d], {"fsdp": dev}).start()

        each(1, NZ, send)
        s1dst[z] = s1src[z]

    def send_u(d):
        q = peer_t(d)
        copy(usend.at[:, q], urecv.at[t], us.at[d], ur.at[d], {"tp": q}).start()

    each(1, NT, send_u)
    urecv[t] = usend[:, t]
    advance(1, 1)

    slot = yl * 2 + core

    @pl.when(carries)
    def _():
        each(1, NZ, lambda d: copy(
            s1src.at[0], s1dst.at[0], s1ss.at[d], s1rs.at[d], {"fsdp": peer_z(d)[1]}).wait_recv())
        rows = permute_rows(
            256,
            lambda r: ((r >> 1) & 7) * 32 + (r >> 4) * 2 + (r & 1),
            s1dst[...].reshape(256, 128),
        )
        s2src[...] = rows.astype(BF).reshape(16, 16, 128)

        def send(d):
            q, dev = peer_p(d)
            copy(s2src.at[q], s2dst.at[slot], s2ss.at[d], s2rs.at[slot], {"fsdp": dev}).start()

        each(1, NP, send)
        s2dst[slot] = s2src[p]

    advance(1, 3)

    each(1, NT, lambda d: copy(
        usend.at[:, 0], urecv.at[0], us.at[d], ur.at[d], {"tp": peer_t(d)}).wait_recv())
    summed = jnp.sum(urecv[...].astype(F32), axis=0).reshape(64, 256)
    u = summed[:, 0:128]
    lane = iota((64, 128), 1)
    sq = jnp.sum(
        jnp.where((lane == 0) | (lane == 64), summed[:, 128:256], 0.0), axis=1, keepdims=True
    )
    inv = lax.rsqrt(sq / D + 1e-06)
    zvals = inv * u + b_ref[...]
    kinv = lax.rsqrt(jnp.sum(zvals * zvals, axis=1, keepdims=True) + 1e-06)
    emb = zvals * kinv

    for i in range(4):
        @pl.when(jnp.logical_not(carries & (slot == i)))
        def _(i=i):
            copy(s2src.at[0], s2dst.at[i], s2ss.at[0], s2rs.at[i], {"fsdp": peer_p(1)[1]}).wait_recv()

    grads = permute_rows(
        64,
        lambda r: ((r >> 5) * 2 + ((r >> 1) & 1)) * 16 + ((r >> 2) & 7) * 2 + (r & 1),
        s2dst[...].reshape(64, 128),
    )
    row = iota((64, 128), 0)
    position = core * 256 + (row >> 5) * 128 + t * 32 + (row & 31)
    grads = jnp.where(position < len_ref[f // 2], grads, 0.0)
    dz = kinv * (grads - emb * jnp.sum(emb * grads, axis=1, keepdims=True))
    cvals = jnp.sum(dz * u, axis=1, keepdims=True)
    coef = inv * inv * inv * cvals / D
    inv_hi, inv_lo = split_hi_lo(inv)
    coef_hi, coef_lo = split_hi_lo(coef)
    tail = jnp.where(
        lane < 64,
        jnp.where(lane < 32, inv_hi, inv_lo),
        jnp.where(lane < 96, coef_hi, coef_lo),
    )
    dzp = dz.astype(BF)
    tailp = tail.astype(BF)
    for i in range(2):
        dzfull[i, t, :, 0:128] = dzp[i * 32 : i * 32 + 32]
        dzfull[i, t, :, 128:256] = tailp[i * 32 : i * 32 + 32]

    def send_dz(d):
        part = dzfull.at[:, t]
        copy(part, part, ds.at[d], dr.at[d], {"tp": peer_t(d)}).start()

    each(1, NT, send_dz)
    advance(3, 6)

    each(1, NT, lambda d: copy(
        dzfull.at[:, 0], dzfull.at[:, 0], ds.at[d], dr.at[d], {"tp": peer_t(d)}).wait_recv())
    dzall = dzfull[:, :, :, 0:128].reshape(256, 128).astype(F32)
    tails = dzfull[:, :, :, 128:256].reshape(256, 128).astype(F32)
    lane = iota((256, 128), 1)
    inv = jnp.sum(jnp.where((lane == 0) | (lane == 32), tails, 0.0), axis=1, keepdims=True)
    coef = jnp.sum(jnp.where((lane == 64) | (lane == 96), tails, 0.0), axis=1, keepdims=True)
    gain = g_ref[...]
    xv = x_ref[...].astype(F32)
    dn = jnp.dot(dzall, p_ref[...], precision=HIGH)
    dh = (inv * gain * dn - xv * coef).astype(BF)
    dhfull[t] = dh.reshape(2, 128, 512)
    tdev = ({"tp": (t + 1) % NT}, {"tp": (t + NT - 1) % NT})

    def dh_move(direction, h):
        part = dhfull.at[t, h]
        return copy(part, part, dhs.at[direction, h], dhr.at[direction, h], tdev[direction])

    for direction, h in ((0, 0), (1, 1), (0, 1), (1, 0)):
        dh_move(direction, h).start()

    xinv = xv * inv
    proj = lax.dot_general(dzall.T, xinv * gain, (((1,), (0,)), ((), ())), precision=HIGH) * (1.0 / 64.0)
    gsum = jnp.sum(dn * xinv, axis=0, keepdims=True) * (1.0 / 64.0)
    bsum = jnp.sum(dzall, axis=0, keepdims=True) * (1.0 / 64.0)
    row8 = iota((8, 128), 0)
    extra = jnp.where(row8 == 4, bsum, 0.0)
    for i in range(4):
        extra = jnp.where(row8 == i, gsum[:, i * 128 : i * 128 + 128], extra)

    def pack_extra(value):
        hi, lo = split_hi_lo(value)
        return jnp.concatenate([hi, lo], axis=0).astype(BF)

    main = jnp.concatenate(
        [proj[:, 0:256].reshape(16, 8, 256), proj[:, 256:512].reshape(16, 8, 256)], axis=1
    )
    rs_src[:, :, 0:256] = main.astype(BF)
    rs_src[:, :, 256:384] = jnp.broadcast_to(pack_extra(extra)[None], (16, 16, 128))

    def send_rs(d):
        q, dev = peer_p(d)
        copy(rs_src.at[q], rs_dst.at[p], rss.at[d], rsr.at[d], {"fsdp": dev}).start()

    each(1, NP, send_rs)
    rs_dst[p] = rs_src[p]
    advance(2, 6)

    def dh_forward(direction):
        part = dhfull.at[(t + NT - 1) % NT if direction == 0 else (t + 1) % NT, direction]
        return copy(part, part, dfs.at[direction], dfr.at[direction], tdev[direction])

    for direction in (0, 1):
        dh_move(direction, direction).wait_recv()
        dh_forward(direction).start()
    advance(2, 4)

    each(1, NP, lambda d: copy(
        rs_src.at[0], rs_dst.at[0], rss.at[d], rsr.at[d], {"fsdp": peer_p(d)[1]}).wait_recv())
    part = jnp.sum(rs_dst[...].astype(F32), axis=0)
    zbuf[z, :, 0:256] = part[:, 0:256].astype(BF)
    zbuf[z, :, 256:384] = pack_extra(part[0:8, 256:384] + part[8:16, 256:384])

    def send_z(d):
        q, dev = peer_z(d)
        copy(zbuf.at[z], zbuf.at[z], zss.at[d], zsr.at[d], {"fsdp": dev}).start()

    each(1, NZ, send_z)
    advance(2, 5)
    each(1, NZ, lambda d: copy(
        zbuf.at[0], zbuf.at[0], zss.at[d], zsr.at[d], {"fsdp": peer_z(d)[1]}).wait_recv())
    part = jnp.sum(zbuf[...].astype(F32), axis=0)
    ag[p] = part[:, 0:256].astype(BF)
    sums = part[0:8, 256:384] + part[8:16, 256:384]
    gain_ref[...] = sums[0:4]
    bias_ref[...] = sums[4:5]

    def send_ag(d):
        q, dev = peer_p(d)
        copy(ag.at[p], ag.at[p], ags.at[d], agr.at[d], {"fsdp": dev}).start()

    each(1, NP, send_ag)
    advance(len(todo0), len(todo1))

    for direction in (0, 1):
        dh_move(direction, 1 - direction).wait_recv()
        dh_forward(direction).wait_recv()
    copy(wfull.at[:, :, :, core], wfull.at[:, :, :, 1 - core], sibs, sibr, {"fsdp": f + 1 - 2 * core}).wait()
    dhv = jnp.concatenate([dhfull[i].reshape(256, 512) for i in range(4)], axis=1)
    for lo, hi in ((0, 512), (512, 1024), (1024, 1408)):
        act_ref[:, lo:hi] = jnp.dot(
            dhv, wfull[:, :, :, :, :, lo:hi].reshape(D, hi - lo), preferred_element_type=F32
        ).astype(BF)

    each(1, NP, lambda d: copy(
        ag.at[0], ag.at[0], ags.at[d], agr.at[d], {"fsdp": peer_p(d)[1]}).wait_recv())
    full = ag[...].astype(F32)
    proj_ref[:, 0:256] = full[:, 0:8].reshape(128, 256)
    proj_ref[:, 256:512] = full[:, 8:16].reshape(128, 256)

    def left_p(d):
        dev = {"fsdp": peer_p(d)[1]}
        copy(rs_src.at[0], rs_dst.at[0], rss.at[d], rsr.at[d], dev).wait_send()
        copy(ag.at[0], ag.at[0], ags.at[d], agr.at[d], dev).wait_send()

    def left_z(d):
        copy(zbuf.at[0], zbuf.at[0], zss.at[d], zsr.at[d], {"fsdp": peer_z(d)[1]}).wait_send()

    def left_t(d):
        dev = {"tp": peer_t(d)}
        copy(usend.at[:, 0], urecv.at[0], us.at[d], ur.at[d], dev).wait_send()
        copy(dzfull.at[:, 0], dzfull.at[:, 0], ds.at[d], dr.at[d], dev).wait_send()

    each(1, NP, left_p)
    each(1, NZ, left_z)
    each(1, NT, left_t)

    @pl.when(carries)
    def _():
        each(1, NZ, lambda d: copy(
            s1src.at[0], s1dst.at[0], s1ss.at[d], s1rs.at[d], {"fsdp": peer_z(d)[1]}).wait_send())
        each(1, NP, lambda d: copy(
            s2src.at[0], s2dst.at[0], s2ss.at[d], s2rs.at[0], {"fsdp": peer_p(d)[1]}).wait_send())

    for direction in (0, 1):
        dh_move(direction, 0).wait_send()
        dh_move(direction, 1).wait_send()
        dh_forward(direction).wait_send()

    @pl.when(core == 0)
    def _():
        for make in sends0:
            make().wait_send()

    @pl.when(core == 1)
    def _():
        for make in sends1:
            make().wait_send()


def shards(token_grads, hidden, proj_weight, proj_bias, norm_gain, down_weight, lengths):
    sem = pltpu.SemaphoreType.DMA
    vmem = pl.BlockSpec(memory_space=pltpu.VMEM)
    act, proj, gain, bias = pl.pallas_call(
        kernel,
        out_shape=(
            jax.ShapeDtypeStruct((256, 1408), BF),
            jax.ShapeDtypeStruct((128, 512), F32),
            jax.ShapeDtypeStruct((4, 128), F32),
            jax.ShapeDtypeStruct((1, 128), F32),
        ),
        in_specs=[vmem] * 6 + [pl.BlockSpec(memory_space=pltpu.SMEM)],
        out_specs=(vmem,) * 4,
        scratch_shapes=[
            pltpu.VMEM((2, NX, NZ, 2, 16, 1408), BF),
            pltpu.VMEM((2, NT, 32, 256), BF),
            pltpu.VMEM((NT, 2, 32, 256), BF),
            pltpu.VMEM((NZ, 32, 128), BF),
            pltpu.VMEM((NZ, 32, 128), BF),
            pltpu.VMEM((NP, 16, 128), BF),
            pltpu.VMEM((4, 16, 128), BF),
            pltpu.VMEM((2, NT, 32, 256), BF),
            pltpu.VMEM((NT, 2, 128, 512), BF),
            pltpu.VMEM((NP, 16, 384), BF),
            pltpu.VMEM((NP, 16, 384), BF),
            pltpu.VMEM((NZ, 16, 384), BF),
            pltpu.VMEM((NP, 16, 256), BF),
            sem((NG,)), sem((NG,)),
            sem((2, 4, 2)), sem((2, 4, 2)),
            sem, sem,
            sem((2, 4)), sem((2, 4)),
            sem((2, 8)), sem((2, 8)),
            sem((8,)), sem((8,)),
            sem, sem,
            sem((NZ,)), sem((NZ,)),
            sem((NP,)), sem((4,)),
            sem((NT,)), sem((NT,)),
            sem((NT,)), sem((NT,)),
            sem((2, 2)), sem((2, 2)),
            sem((2,)), sem((2,)),
            sem((NP,)), sem((NP,)),
            sem((NZ,)), sem((NZ,)),
            sem((NP,)), sem((NP,)),
        ],
        compiler_params=pltpu.CompilerParams(
            collective_id=0, has_side_effects=True, vmem_limit_bytes=48 * 1024 * 1024
        ),
    )(
        token_grads, hidden, proj_weight, proj_bias.reshape(1, 128), norm_gain.reshape(1, 512),
        down_weight.T, lengths,
    )
    return act, proj, gain.reshape(512), bias.reshape(128)


def solution(mesh):
    placed = (P("fsdp", None), P("fsdp", "tp"), P(None, "tp"), P(), P("tp"), P("tp", "fsdp"), P())
    return jax.shard_map(
        shards,
        mesh=mesh,
        in_specs=placed,
        out_specs=(P("fsdp", "tp"), P(None, "tp"), P("tp"), P()),
        check_vma=False,
    )
```

time: 1300 us -> 73.3 us (0.06)
  waiting for transfers between devices: 960 us -> 0 us
  blocking collectives: 289 us -> 0 us
  Pallas kernels: 0 us -> 65.4 us
  starting transfers between devices: 16.8 us -> 0 us
  between operations: 13.8 us -> 0.67 us
    psum x2 -> x0, waiting for transfers between devices: 705 us -> none  [the longest x1 677 us: shards(): lax.psum((proj_part, gain_part, bias_part), 'fsdp')]
    psum x2 -> x0, blocking collectives: 289 us -> none  [the longest x1 278 us: shards(): lax.psum((proj_part, gain_part, bias_part), 'fsdp')]
    all_gather x2 -> x0, waiting for transfers between devices: 255 us -> none  [the longest x1 221 us: shards(): full_down = lax.all_gather(down_low, 'fsdp', axis=1, tiled=True)]
    pallas_call x0 -> x1, Pallas kernels: none -> 65.4 us  [shards(): pl.pallas_call(kernel, out_shape=(jax.ShapeDtypeStruct((256, 1408), BF),...]
    all_to_all x1 -> x0, starting transfers between devices: 16.6 us -> none  [shards(): lax.all_to_all(shaped.astype(jnp.bfloat16), 'fsdp', split_axis=0, concat_...]
  transfers between devices with their start and end apart: 5 -> 0, of which waited for: 4 -> 0; matrix products, arithmetic and copies ran while one was open for 1% -> 0% of each run, Pallas kernels for 0% -> 0%
where the time goes in v1:
time: 73.3 us; the launch traced here: 73.1 us
  Pallas kernels  65.4 us (89%)
  local copies, waits for them, and re-layouts  7.01 us (10%)
    pallas_call x1, Pallas kernels, shards(): pl.pallas_call(kernel, out_shape=(jax.ShapeDtypeStruct((256, 1408), BF),...  65.4 us
    unnamed x18, local copies, waits for them, and re-layouts  7.01 us

profile of v1, /device:TPU:1, one launch (start us, length us, event | category | flops | bytes accessed | tf_op | source)
XLA Modules:
  0.0 73.1 jit_solution(13264043278796985470)
XLA Ops:
  0.6 0.0 copy-start.4
  0.6 0.0 copy-start.5
  0.7 0.0 copy-start.6
  0.7 0.7 copy-done.4
  1.3 0.0 copy-done.5
  1.3 0.0 copy-done.6
  1.3 0.0 copy-start
  1.3 0.9 %copy-done = bf16[256,512]{1,0:T(8,128)(2,1)S(1)} copy-done((bf16[256,512]{1,0:T(8,128)(2,1)S(1)}, bf16[256,512]{1,0:T(8,128)(2,1)}, u32[]{:S(2)}) %copy-start) | copy-done | bytes 262168
  2.3 0.0 copy-start.1
  2.3 0.9 %copy-done.1 = f32[128,512]{1,0:T(8,128)S(1)} copy-done((f32[128,512]{1,0:T(8,128)S(1)}, f32[128,512]{1,0:T(8,128)}, u32[]{:S(2)}) %copy-start.1) | copy-done | bytes 262168
  3.2 0.0 copy-start.2
  3.2 0.9 %copy-done.2 = f32[256,128]{1,0:T(8,128)S(1)} copy-done((f32[256,128]{1,0:T(8,128)S(1)}, f32[256,128]{1,0:T(8,128)}, u32[]{:S(2)}) %copy-start.2) | copy-done | bytes 131096
  4.1 0.0 copy-start.3
  4.1 0.9 %copy-done.3 = f32[1408,16]{0,1:T(8,128)S(1)} copy-done((f32[1408,16]{0,1:T(8,128)S(1)}, f32[1408,16]{0,1:T(8,128)}, u32[]{:S(2)}) %copy-start.3) | copy-done | bytes 90136
  5.0 65.4 %shard_map.102 = (bf16[256,1408]{1,0:T(8,128)(2,1)S(1)}, f32[128,512]{1,0:T(8,128)S(1)}, f32[4,128]{1,0:T(4,128)S(1)}, f32[1,128]{1,0:T(1,128)S(1)}) custom-call(f32[256,128]{1,0:T(8,128)S(1)} %copy-done.2, bf16[256,512]{1,0:T(8,128)(2,1)S(1)} %copy-done, f32[128,512]{1,0:T(8,128)S(1)} %copy-done.1, f32[1,128]{1,0:T(1,128)S(1)} %bitcast.8, ...), custom_call_target="tpu_custom_call" | custom-call | tf_op jit(solution)/shard_map/pallas_call | solution.py:485
  70.4 0.9 %copy.15 = bf16[256,1408]{1,0:T(8,128)(2,1)} copy(bf16[256,1408]{1,0:T(8,128)(2,1)S(1)} %get-tuple-element.16) | data formatting | bytes 1441792
  71.3 0.7 copy.16
  72.0 0.6 copy.17
  72.6 0.5 copy.18
Async XLA Ops:
  0.6 0.7 copy-start.4
  0.6 0.7 copy-start.5
  0.7 0.7 copy-start.6
  1.3 1.0 %copy-start = (bf16[256,512]{1,0:T(8,128)(2,1)S(1)}, bf16[256,512]{1,0:T(8,128)(2,1)}, u32[]{:S(2)}) copy-start(bf16[256,512]{1,0:T(8,128)(2,1)} %x_ref.1) | copy-start | bytes 786436
  2.3 0.9 %copy-start.1 = (f32[128,512]{1,0:T(8,128)S(1)}, f32[128,512]{1,0:T(8,128)}, u32[]{:S(2)}) copy-start(f32[128,512]{1,0:T(8,128)} %p_ref.1) | copy-start | bytes 786436
  3.2 0.9 %copy-start.2 = (f32[256,128]{1,0:T(8,128)S(1)}, f32[256,128]{1,0:T(8,128)}, u32[]{:S(2)}) copy-start(f32[256,128]{1,0:T(8,128)} %tg_ref.1) | copy-start | bytes 393220
  4.1 0.9 %copy-start.3 = (f32[1408,16]{0,1:T(8,128)S(1)}, f32[1408,16]{0,1:T(8,128)}, u32[]{:S(2)}) copy-start(f32[1408,16]{0,1:T(8,128)} %param.12) | copy-start | bytes 270340

commit v2 on v1

v2 whole, which is shorter than its diff:
```python
import jax
import jax.numpy as jnp
from jax import lax
from jax.experimental import pallas as pl
from jax.experimental.pallas import tpu as pltpu
from jax.sharding import PartitionSpec as P

D = 2048
LEN = 512
NX, NZ, NG, NP, NT = 4, 8, 8, 16, 4
HIDL, HIDP = 1408, 1536
YREC, XREC = 28, {1: 29, 2: 30, 3: 31, 5: 56, 6: 57, 7: 58}
VLIM = 56 * 1024 * 1024
MESH = pl.DeviceIdType.MESH
HIGH = lax.Precision.HIGHEST
BF, F32, I32 = jnp.bfloat16, jnp.float32, jnp.int32
NT_DIMS = (((1,), (1,)), ((), ()))


def iota(shape, axis):
    return lax.broadcasted_iota(I32, shape, axis)


def split_hi_lo(value):
    hi = value.astype(BF).astype(F32)
    return hi, value - hi


def permute_rows(count, source_of, rows):
    hot = jnp.where(
        iota((count, count), 1) == source_of(iota((count, count), 0)), F32(1.0), F32(0.0)
    ).astype(BF)
    return jnp.dot(hot, rows, preferred_element_type=F32)


def kernel(
    tg_hbm, x_hbm, p_hbm, b_hbm, g_hbm, w_hbm, len_hbm,
    act_out, proj_out, gain_out, bias_out,
    act_ref, proj_ref, gain_ref, bias_ref, outs,
    tg_ref, xfull, p_ref, b_ref, g_ref, w_ref, len_ref,
    wfull, pgt, usend, urecv, s1src, s1dst, s2src, s2dst, dzfull, dhv, rs_src, rs_dst, zbuf, ag,
    ins, ringsend, sidesend, wr, sibs, sibr,
    s1ss, s1rs, s2ss, s2rs, us, ur, ps, pr, ds, dr, dhs, dhr, dfr, rss, rsr, zss, zsr, ags, agr,
):
    f = lax.axis_index("fsdp")
    t = lax.axis_index("tp")
    core = f % 2
    z = (f // 2) % NZ
    grp = f // 16
    xa = grp % NX
    yl = grp // NX
    p = f % 16

    def at_f(group, zpos, cpos):
        return group * 16 + zpos * 2 + cpos

    def peer_p(d):
        q = (p + d) % NP
        return q, grp * 16 + q

    def peer_g(d):
        q = (grp + d) % NG
        return q, q * 16 + p

    def peer_t(d):
        return (t + d) % NT

    def copy(src, dst, ssem, rsem, dev):
        return pltpu.make_async_remote_copy(
            src_ref=src, dst_ref=dst, send_sem=ssem, recv_sem=rsem,
            device_id=dev, device_id_type=MESH,
        )

    def each(lo, hi, body):
        def step(d, carry):
            body(d)
            return carry

        lax.fori_loop(lo, hi, step, 0)

    loads = [
        pltpu.make_async_copy(src, dst, ins.at[i])
        for i, (src, dst) in enumerate((
            (w_hbm, w_ref), (tg_hbm, tg_ref), (x_hbm, xfull.at[t]), (p_hbm, p_ref),
            (g_hbm, g_ref), (b_hbm, b_ref), (len_hbm, len_ref),
        ))
    ]
    for load in loads:
        load.start()

    near_p = {"fsdp": peer_p(1)[1]}
    near_g = {"fsdp": peer_g(1)[1]}

    bar = pltpu.get_barrier_semaphore()

    def greet(dev):
        pl.semaphore_signal(bar, inc=1, device_id=dev, device_id_type=MESH)

    each(1, NP, lambda d: greet({"fsdp": peer_p(d)[1]}))
    each(1, NG, lambda d: greet({"fsdp": peer_g(d)[1]}))
    each(1, NT, lambda d: greet({"tp": peer_t(d)}))

    loads[0].wait()
    wfull[yl, xa, z, core, :, 0:HIDL] = w_ref[...].astype(BF)
    loads[1].wait()
    carries = grp // 2 == t

    @pl.when(carries)
    def _():
        rows = permute_rows(
            256, lambda r: ((r >> 1) & 7) * 32 + (r >> 4) * 2 + (r & 1), tg_ref[...].astype(BF)
        )
        s1src[...] = rows.astype(BF).reshape(16, 16, 128)

    for load in loads[2:]:
        load.wait()
    gain = g_ref[...]
    pg = p_ref[...] * gain
    pg_hi = pg.astype(BF)
    pg_lo = (pg - pg_hi.astype(F32)).astype(BF)
    pgt[...] = pg.T.astype(BF).reshape(32, 16, 128)
    pl.semaphore_wait(bar, (NP - 1) + (NG - 1) + (NT - 1))

    def go(make):
        make().start()

    def sibling(piece):
        copy(piece, piece, sibs, sibr, {"fsdp": f + 1 - 2 * core}).start()

    own = wfull.at[yl, xa, z, core]
    met = wfull.at[1 - yl, xa, z, core]
    own_p = wfull.at[yl, xa, z, core, :, pl.ds(HIDL, 128)]
    zdev = ({"fsdp": at_f(grp, (z + 1) % NZ, core)}, {"fsdp": at_f(grp, (z + NZ - 1) % NZ, core)})
    xdev = (
        {"fsdp": at_f(yl * NX + (xa + 1) % NX, z, core)},
        {"fsdp": at_f(yl * NX + (xa + NX - 1) % NX, z, core)},
    )

    ydev = {"fsdp": at_f((grp + NX) % NG, z, core)}

    def zslot(direction, s):
        return (z + NZ - s) % NZ if direction == 0 else (z + s) % NZ

    def piece0(i, zj):
        return wfull.at[yl if i < NX else 1 - yl, (xa + i % NX) % NX, zj, 0]

    def xdev_at(d):
        return {"fsdp": at_f(yl * NX + (xa + d) % NX, z, core)}

    def zmove0(direction, s, i):
        def make():
            piece = piece0(i, zslot(direction, s))
            return copy(piece, piece, ringsend, wr.at[direction * 32 + s * 8 + i], zdev[direction])

        return make

    def launch0(i):
        for direction in (0, 1):
            go(zmove0(direction, 0, i))
        sibling(piece0(i, z))

    def begin0():
        go(lambda: copy(own, own, sidesend, wr.at[YREC], ydev))
        for d in range(1, NX):
            go(lambda d=d: copy(own, own, sidesend, wr.at[XREC[d]], xdev_at(NX - d)))
        launch0(0)

    def relay0():
        copy(met, met, sidesend, wr.at[YREC], ydev).wait_recv()
        for d in range(1, NX):
            go(lambda d=d: copy(met, met, sidesend, wr.at[XREC[NX + d]], xdev_at(NX - d)))
        launch0(NX)

    def ring0(i):
        def run():
            copy(own, own, sidesend, wr.at[XREC[i]], zdev[0]).wait_recv()
            launch0(i)

        return run

    def arrive0(s, direction, i):
        zmove0(direction, s - 1, i)().wait_recv()
        if s < 3 or (s == 3 and (i < NX) == (direction == 0)):
            go(zmove0(direction, s, i))
        sibling(piece0(i, zslot(direction, s)))

    def step0(s, i):
        def run():
            if s < 4 or i < NX:
                arrive0(s, 0, i)
            if s < 4:
                arrive0(s, 1, i)
            elif i < NX:
                arrive0(s, 1, i + NX)

        return run

    todo0 = [begin0, ring0(1), ring0(3), ring0(2), relay0, step0(1, 0), ring0(5), ring0(7), ring0(6)]
    order = (1, 3, 2, 4, 5, 7, 6)
    todo0 += [step0(1, i) for i in order]
    todo0 += [step0(2, i) for i in (0,) + order] + [step0(3, i) for i in (0,) + order]
    todo0 += [step0(4, i) for i in (0, 1, 3, 2)]

    hops = [(0, 0), (0, 1), (1, 1), (0, 2), (1, 2), (0, 3), (1, 3), (0, 4)]

    def piece1(xj, zj):
        return wfull.at[:, xj, zj, 1]

    def zmove1(direction, s):
        def make():
            piece = piece1(xa, zslot(direction, s))
            return copy(piece, piece, ringsend, wr.at[direction * 4 + s], zdev[direction])

        return make

    def xmove(direction, k):
        def make():
            piece = piece1(xa, zslot(*hops[k]))
            return copy(piece, piece, sidesend, wr.at[8 + direction * 8 + k], xdev[direction])

        return make

    def xforward(k):
        direction = k % 2

        def make():
            xj = (xa + NX - 1) % NX if direction == 0 else (xa + 1) % NX
            piece = piece1(xj, zslot(*hops[k]))
            return copy(piece, piece, sidesend, wr.at[24 + k], xdev[direction])

        return make

    def begin1():
        go(lambda: copy(own, own, ringsend, wr.at[32], ydev))

    def spread(k):
        go(xmove(0, k))
        go(xmove(1, k))
        sibling(piece1(xa, zslot(*hops[k])))

    def first1():
        copy(met, met, ringsend, wr.at[32], ydev).wait_recv()
        go(zmove1(0, 0))
        go(zmove1(1, 0))
        spread(0)

    def zstep1(k):
        def run():
            direction, s = hops[k]
            zmove1(direction, s - 1)().wait_recv()
            if s < 3 or (s == 3 and direction == 0):
                go(zmove1(direction, s))
            spread(k)

        return run

    def xstep1(k, direction):
        def run():
            xmove(direction, k)().wait_recv()
            xj = (xa + NX - 1) % NX if direction == 0 else (xa + 1) % NX
            if k % 2 == direction:
                go(xforward(k))
            sibling(piece1(xj, zslot(*hops[k])))

        return run

    def fstep1(k):
        def run():
            xforward(k)().wait_recv()
            sibling(piece1((xa + 2) % NX, zslot(*hops[k])))

        return run

    todo1 = [begin1, first1]
    for k in range(1, 8):
        todo1.append(zstep1(k))
        if k >= 3:
            todo1 += [xstep1(k - 3, 0), xstep1(k - 3, 1)]
        if k >= 6:
            todo1.append(fstep1(k - 6))
    for k in (5, 6, 7):
        todo1 += [xstep1(k, 0), xstep1(k, 1), fstep1(k - 3)]
    todo1 += [fstep1(k) for k in (5, 6, 7)]

    def advance(n0, n1):
        head0, head1 = todo0[:n0], todo1[:n1]
        del todo0[:n0], todo1[:n1]
        if head0:
            @pl.when(core == 0)
            def _():
                for run in head0:
                    run()
        if head1:
            @pl.when(core == 1)
            def _():
                for run in head1:
                    run()

    p_slab = f // 32
    p_row = f % 32
    p_src = pgt.at[p_row]

    @pl.when(p_slab == t)
    def _():
        def send(d):
            copy(p_src, own_p, ps, pr, {"tp": peer_t(d)}).start()

        each(1, NT, send)
        wfull[yl, xa, z, core, :, HIDL:HIDP] = pgt[p_row]

    @pl.when(carries)
    def _():
        def send(d):
            q, dev = peer_p(d)
            copy(s1src.at[q], s1dst.at[p], s1ss, s1rs, {"fsdp": dev}).start()

        each(1, NP, send)
        s1dst[p] = s1src[p]

    xv = xfull[t].reshape(256, 512)
    pu = lax.dot_general(xv, pg_hi, NT_DIMS, preferred_element_type=F32)
    pu = pu + lax.dot_general(xv, pg_lo, NT_DIMS, preferred_element_type=F32)
    xv = xv.astype(F32)
    sq_hi, sq_lo = split_hi_lo(jnp.sum(xv * xv, axis=1, keepdims=True))
    sq2 = jnp.where(iota((256, 128), 1) < 64, sq_hi, sq_lo)
    usend[:, :, 0:128] = pu.astype(BF).reshape(4, 64, 128)
    usend[:, :, 128:256] = sq2.astype(BF).reshape(4, 64, 128)

    def send_u(d):
        q = peer_t(d)
        copy(usend.at[q], urecv.at[t], us, ur, {"tp": q}).start()

    each(1, NT, send_u)
    urecv[t] = usend[t]

    tdev = ({"tp": (t + 1) % NT}, {"tp": (t + NT - 1) % NT})

    def x_move(direction, h):
        part = xfull.at[t, h]
        return copy(part, part, dhs, dhr.at[direction, h], tdev[direction])

    def x_forward(direction):
        part = xfull.at[(t + NT - 1) % NT if direction == 0 else (t + 1) % NT, direction]
        return copy(part, part, dhs, dfr.at[direction], tdev[direction])

    @pl.when(p_slab != t)
    def _():
        copy(p_src, own_p, ps, pr, tdev[0]).wait_recv()

    advance(1, 1)

    slot = grp % 2

    @pl.when(carries)
    def _():
        copy(s1src.at[0:15], s1dst.at[0:15], s1ss, s1rs, near_p).wait_recv()
        rows = permute_rows(
            256,
            lambda r: ((r >> 1) & 15) * 16 + (r >> 5) * 2 + (r & 1),
            s1dst[...].reshape(256, 128),
        )
        s2src[...] = rows.astype(BF).reshape(8, 32, 128)

        def send(d):
            q, dev = peer_g(d)
            copy(s2src.at[q], s2dst.at[slot], s2ss, s2rs.at[slot], {"fsdp": dev}).start()

        each(1, NG, send)
        s2dst[slot] = s2src[grp]

    advance(3, 1)

    copy(usend.at[0:3], urecv.at[0:3], us, ur, tdev[0]).wait_recv()
    summed = jnp.sum(urecv[...].astype(F32), axis=0)
    u = summed[:, 0:128]
    lane = iota((64, 128), 1)
    sq = jnp.sum(
        jnp.where((lane == 0) | (lane == 64), summed[:, 128:256], 0.0), axis=1, keepdims=True
    )
    inv = lax.rsqrt(sq / D + 1e-06)
    zvals = inv * u + b_ref[...]
    kinv = lax.rsqrt(jnp.sum(zvals * zvals, axis=1, keepdims=True) + 1e-06)
    emb = zvals * kinv
    advance(0, 1)

    for i in range(2):
        @pl.when(jnp.logical_not(carries & (slot == i)))
        def _(i=i):
            copy(s2src.at[0], s2dst.at[i], s2ss, s2rs.at[i], {"fsdp": peer_g(1)[1]}).wait_recv()

    position = core * 256 + t * 64 + iota((64, 128), 0)
    grads = jnp.where(
        position < len_ref[f // 2], s2dst[...].reshape(64, 128).astype(F32), 0.0
    )
    dz = kinv * (grads - emb * jnp.sum(emb * grads, axis=1, keepdims=True))
    cvals = jnp.sum(dz * u, axis=1, keepdims=True)
    coef = inv * inv * inv * cvals / D
    inv_hi, inv_lo = split_hi_lo(inv)
    coef_hi, coef_lo = split_hi_lo(coef)
    tail = jnp.where(
        lane < 64,
        jnp.where(lane < 32, inv_hi, inv_lo),
        jnp.where(lane < 96, coef_hi, coef_lo),
    )
    dzfull[t, :, 0:128] = dz.astype(BF)
    dzfull[t, :, 128:256] = tail.astype(BF)

    def send_dz(d):
        part = dzfull.at[t]
        copy(part, part, ds, dr, {"tp": peer_t(d)}).start()

    each(1, NT, send_dz)
    advance(12, 2)

    copy(dzfull.at[0:3], dzfull.at[0:3], ds, dr, tdev[0]).wait_recv()
    dzall = dzfull[:, :, 0:128].reshape(256, 128)
    tails = dzfull[:, :, 128:256].reshape(256, 128).astype(F32)
    lane = iota((256, 128), 1)
    inv = jnp.sum(jnp.where((lane == 0) | (lane == 32), tails, 0.0), axis=1, keepdims=True)
    coef = jnp.sum(jnp.where((lane == 64) | (lane == 96), tails, 0.0), axis=1, keepdims=True)
    dzf = dzall.astype(F32)
    xinv = (xfull[t].reshape(256, 512).astype(F32) * (inv * (1.0 / 64.0))).astype(BF)
    sums = jnp.dot(dzf.T.astype(BF), xinv, preferred_element_type=F32)
    bsum = jnp.sum(dzf, axis=0, keepdims=True) * (1.0 / 64.0)
    row8 = iota((8, 128), 0)
    extra = jnp.where(row8 == 0, bsum, 0.0)

    def pack_extra(value):
        hi, lo = split_hi_lo(value)
        return jnp.concatenate([hi, lo], axis=0).astype(BF)

    main = jnp.concatenate(
        [sums[:, 0:256].reshape(16, 8, 256), sums[:, 256:512].reshape(16, 8, 256)], axis=1
    )
    rs_src[:, :, 0:256] = main.astype(BF)
    rs_src[:, :, 256:384] = jnp.broadcast_to(pack_extra(extra)[None], (16, 16, 128))

    def send_rs(d):
        q, dev = peer_p(d)
        copy(rs_src.at[q], rs_dst.at[p], rss, rsr, {"fsdp": dev}).start()

    each(1, NP, send_rs)
    rs_dst[p] = rs_src[p]
    for direction, h in ((0, 0), (1, 1), (0, 1), (1, 0)):
        x_move(direction, h).start()
    advance(8, 9)
    for direction in (0, 1):
        x_move(direction, direction).wait_recv()
        x_forward(direction).start()
    advance(4, 11)

    copy(rs_src.at[0:15], rs_dst.at[0:15], rss, rsr, near_p).wait_recv()
    part = jnp.sum(rs_dst[...].astype(F32), axis=0)
    zbuf[grp, :, 0:256] = part[:, 0:256].astype(BF)
    zbuf[grp, :, 256:384] = pack_extra(part[0:8, 256:384] + part[8:16, 256:384])

    def send_z(d):
        q, dev = peer_g(d)
        copy(zbuf.at[grp], zbuf.at[grp], zss, zsr, {"fsdp": dev}).start()

    each(1, NG, send_z)
    advance(4, 4)
    copy(zbuf.at[0:7], zbuf.at[0:7], zss, zsr, near_g).wait_recv()
    part = jnp.sum(zbuf[...].astype(F32), axis=0)
    ag[p] = part[:, 0:256].astype(BF)
    bias_ref[...] = (part[0:8, 256:384] + part[8:16, 256:384])[0:1]

    def send_ag(d):
        q, dev = peer_p(d)
        copy(ag.at[p], ag.at[p], ags, agr, {"fsdp": dev}).start()

    each(1, NP, send_ag)
    advance(len(todo0), len(todo1))

    for direction in (0, 1):
        x_move(direction, 1 - direction).wait_recv()
        x_forward(direction).wait_recv()
    copy(wfull.at[:, :, :, core], wfull.at[:, :, :, 1 - core], sibs, sibr, {"fsdp": f + 1 - 2 * core}).wait()
    for j in range(NT):
        for k in range(2):
            pgt_part = wfull[j // 2, (j % 2) * 2 + k, :, :, :, HIDL:HIDP].reshape(256, 128)
            dn = lax.dot_general(dzall, pgt_part, NT_DIMS, preferred_element_type=F32)
            xpart = xfull[j, :, :, k * 256 : k * 256 + 256].reshape(256, 256).astype(F32)
            lo = j * 512 + k * 256
            dhv[:, lo : lo + 256] = (inv * dn - xpart * coef).astype(BF)
    stores = []

    def store(src, dst):
        move = pltpu.make_async_copy(src, dst, outs.at[len(stores)])
        move.start()
        stores.append(move)

    store(bias_ref, bias_out)
    for lo, hi in ((0, 512), (512, 1024), (1024, 1408)):
        act_ref[:, lo:hi] = jnp.dot(
            dhv[...], wfull[:, :, :, :, :, lo:hi].reshape(D, hi - lo), preferred_element_type=F32
        ).astype(BF)
        store(act_ref.at[:, lo:hi], act_out.at[:, lo:hi])

    copy(rs_src.at[0:15], rs_dst.at[0:15], rss, rsr, near_p).wait_send()
    copy(zbuf.at[0:7], zbuf.at[0:7], zss, zsr, near_g).wait_send()
    copy(usend.at[0:3], urecv.at[0:3], us, ur, tdev[0]).wait_send()
    copy(dzfull.at[0:3], dzfull.at[0:3], ds, dr, tdev[0]).wait_send()
    copy(xfull.at[0:3], xfull.at[0:3], dhs, dfr.at[0], tdev[0]).wait_send()

    @pl.when(p_slab == t)
    def _():
        copy(pgt.at[0:3], pgt.at[0:3], ps, pr, tdev[0]).wait_send()

    @pl.when(carries)
    def _():
        copy(s1src.at[0:15], s1dst.at[0:15], s1ss, s1rs, near_p).wait_send()
        copy(s2src.at[0:7], s2src.at[0:7], s2ss, s2rs.at[0], near_g).wait_send()

    def all_left(part, send_sem):
        copy(part, part, send_sem, wr.at[0], zdev[0]).wait_send()

    @pl.when(core == 0)
    def _():
        all_left(wfull.at[:, :, 0:7, 0], ringsend)
        all_left(wfull.at[0, 0, 0:7, 0], sidesend)

    @pl.when(core == 1)
    def _():
        all_left(wfull.at[0, 0:3, 0:5, 1], ringsend)
        all_left(wfull.at[:, 0:3, :, 1], sidesend)

    copy(ag.at[0:15], ag.at[0:15], ags, agr, near_p).wait()
    full = ag[...].astype(F32)
    full = jnp.concatenate(
        [full[:, 0:8].reshape(128, 256), full[:, 8:16].reshape(128, 256)], axis=1
    )
    proj_ref[...] = full * gain
    gain_ref[...] = jnp.sum(full * p_ref[...], axis=0, keepdims=True)
    store(proj_ref, proj_out)
    store(gain_ref, gain_out)

    for move in stores:
        move.wait()


def shards(token_grads, hidden, proj_weight, proj_bias, norm_gain, down_weight, lengths):
    sem = pltpu.SemaphoreType.DMA
    anywhere = pl.BlockSpec(memory_space=pl.ANY)
    results = (
        jax.ShapeDtypeStruct((256, HIDL), BF),
        jax.ShapeDtypeStruct((128, 512), F32),
        jax.ShapeDtypeStruct((1, 512), F32),
        jax.ShapeDtypeStruct((1, 128), F32),
    )
    act, proj, gain, bias = pl.pallas_call(
        kernel,
        out_shape=results,
        in_specs=[anywhere] * 7,
        out_specs=(anywhere,) * 4,
        scratch_shapes=[
            pltpu.VMEM((256, HIDL), BF),
            pltpu.VMEM((128, 512), F32),
            pltpu.VMEM((1, 512), F32),
            pltpu.VMEM((1, 128), F32),
            sem((6,)),
            pltpu.VMEM((256, 128), F32),
            pltpu.VMEM((NT, 2, 128, 512), BF),
            pltpu.VMEM((128, 512), F32),
            pltpu.VMEM((1, 128), F32),
            pltpu.VMEM((1, 512), F32),
            pltpu.VMEM((16, HIDL), F32),
            pltpu.SMEM((64,), I32),
            pltpu.VMEM((2, NX, NZ, 2, 16, HIDP), BF),
            pltpu.VMEM((32, 16, 128), BF),
            pltpu.VMEM((NT, 64, 256), BF),
            pltpu.VMEM((NT, 64, 256), BF),
            pltpu.VMEM((NP, 16, 128), BF),
            pltpu.VMEM((NP, 16, 128), BF),
            pltpu.VMEM((NG, 32, 128), BF),
            pltpu.VMEM((2, 32, 128), BF),
            pltpu.VMEM((NT, 64, 256), BF),
            pltpu.VMEM((256, D), BF),
            pltpu.VMEM((NP, 16, 384), BF),
            pltpu.VMEM((NP, 16, 384), BF),
            pltpu.VMEM((NG, 16, 384), BF),
            pltpu.VMEM((NP, 16, 256), BF),
            sem((7,)),
            sem, sem, sem((64,)), sem, sem,
            sem, sem, sem, sem((2,)),
            sem, sem, sem, sem,
            sem, sem,
            sem, sem((2, 2)), sem((2,)),
            sem, sem, sem, sem, sem, sem,
        ],
        compiler_params=pltpu.CompilerParams(
            collective_id=0, has_side_effects=True, vmem_limit_bytes=VLIM
        ),
    )(
        token_grads, hidden.reshape(2, 128, 512), proj_weight, proj_bias.reshape(1, 128),
        norm_gain.reshape(1, 512), down_weight.T, lengths,
    )
    return act, proj, gain.reshape(512), bias.reshape(128)


def solution(mesh):
    placed = (P("fsdp", None), P("fsdp", "tp"), P(None, "tp"), P(), P("tp"), P("tp", "fsdp"), P())
    return jax.shard_map(
        shards,
        mesh=mesh,
        in_specs=placed,
        out_specs=(P("fsdp", "tp"), P(None, "tp"), P("tp"), P()),
        check_vma=False,
    )
```

time: 73.3 us -> 64 us (0.87)
  Pallas kernels: 65.4 us -> 59.3 us
  local copies, waits for them, and re-layouts: 7.01 us -> 3.89 us
    pallas_call x1, Pallas kernels: 65.4 us -> 59.3 us  [shards(): pl.pallas_call(kernel, out_shape=results, in_specs=[anywhere] * 7, out_sp...]
    unnamed x18 -> x10, local copies, waits for them, and re-layouts: 7.01 us -> 3.89 us
where the time goes in v2:
time: 64 us; the launch traced here: 63.8 us
  Pallas kernels  59.3 us (93%)
  local copies, waits for them, and re-layouts  3.89 us (6%)
  between operations  0.65 us (1%)
    pallas_call x1, Pallas kernels, shards(): pl.pallas_call(kernel, out_shape=results, in_specs=[anywhere] * 7, out_sp...  59.3 us
    unnamed x10, local copies, waits for them, and re-layouts  3.89 us

profile of v2, /device:TPU:1, one launch (start us, length us, event | category | flops | bytes accessed | tf_op | source)
XLA Modules:
  0.0 63.8 jit_solution(1403783106978377766)
XLA Ops:
  0.6 59.3 %shard_map.102 = (bf16[256,1408]{1,0:T(8,128)(2,1)}, f32[128,512]{1,0:T(8,128)}, f32[1,512]{1,0:T(1,128)}, f32[1,128]{1,0:T(1,128)}) custom-call(f32[256,128]{1,0:T(8,128)} %tg_hbm.1, bf16[2,128,512]{2,1,0:T(8,128)(2,1)} %bitcast.6, f32[128,512]{1,0:T(8,128)} %p_hbm.1, f32[1,128]{1,0:T(1,128)} %bitcast.10, f32[1,512]{1,0:T(1,128)} %bitcast.8, ...), custom_call_target="tpu_custom_call" | custom-call | tf_op jit(solution)/shard_map/pallas_call | solution.py:551
  59.9 0.0 copy-start
  59.9 2.1 %copy.15 = bf16[256,1408]{1,0:T(8,128)(2,1)} copy(bf16[256,1408]{1,0:T(8,128)(2,1)} %get-tuple-element.16) | data formatting | bytes 1441792
  62.0 0.0 copy-done
  62.0 0.0 copy-start.1
  62.0 0.7 %copy.16 = f32[128,512]{1,0:T(8,128)} copy(f32[128,512]{1,0:T(8,128)S(1)} %copy-done) | data formatting | bytes 524288
  62.7 0.0 copy-done.1
  62.7 0.0 copy-start.2
  62.7 0.6 copy.17
  63.3 0.0 copy-done.2
  63.3 0.5 copy.18
Async XLA Ops:
  59.9 2.1 %copy-start = (f32[128,512]{1,0:T(8,128)S(1)}, f32[128,512]{1,0:T(8,128)}, u32[]{:S(2)}) copy-start(f32[128,512]{1,0:T(8,128)} %get-tuple-element.17) | copy-start | bytes 786436
  62.0 0.7 %copy-start.1 = (f32[1,512]{1,0:T(1,128)S(1)}, f32[1,512]{1,0:T(1,128)}, u32[]{:S(2)}) copy-start(f32[1,512]{1,0:T(1,128)} %get-tuple-element.10) | copy-start | bytes 6148
  62.7 0.6 copy-start.2

commit v3 on v2

--- a/solution.py
+++ b/solution.py
@@ -129,6 +129,9 @@
 
     own = wfull.at[yl, xa, z, core]
     met = wfull.at[1 - yl, xa, z, core]
+    met_w = wfull.at[1 - yl, xa, z, core, :, pl.ds(0, HIDL)]
+    met_p = wfull.at[1 - yl, xa, z, core, :, pl.ds(HIDL, 128)]
+    own_w = wfull.at[yl, xa, z, core, :, pl.ds(0, HIDL)]
     own_p = wfull.at[yl, xa, z, core, :, pl.ds(HIDL, 128)]
     zdev = ({"fsdp": at_f(grp, (z + 1) % NZ, core)}, {"fsdp": at_f(grp, (z + NZ - 1) % NZ, core)})
     xdev = (
@@ -159,17 +162,27 @@
             go(zmove0(direction, 0, i))
         sibling(piece0(i, z))
 
-    def begin0():
-        go(lambda: copy(own, own, sidesend, wr.at[YREC], ydev))
+    def begin0(part, yrec):
+        go(lambda: copy(part, part, sidesend, wr.at[yrec], ydev))
         for d in range(1, NX):
-            go(lambda d=d: copy(own, own, sidesend, wr.at[XREC[d]], xdev_at(NX - d)))
-        launch0(0)
-
-    def relay0():
-        copy(met, met, sidesend, wr.at[YREC], ydev).wait_recv()
+            go(lambda d=d: copy(part, part, sidesend, wr.at[XREC[d]], xdev_at(NX - d)))
+        for direction in (0, 1):
+            go(lambda: copy(part, part, ringsend, wr.at[direction * 32], zdev[direction]))
+
+    def end_begin0():
+        begin0(own_p, YREC + 31)
+        sibling(own)
+
+    def relay0(part, yrec):
+        copy(part, part, sidesend, wr.at[yrec], ydev).wait_recv()
         for d in range(1, NX):
-            go(lambda d=d: copy(met, met, sidesend, wr.at[XREC[NX + d]], xdev_at(NX - d)))
-        launch0(NX)
+            go(lambda d=d: copy(part, part, sidesend, wr.at[XREC[NX + d]], xdev_at(NX - d)))
+        for direction in (0, 1):
+            go(lambda: copy(part, part, ringsend, wr.at[direction * 32 + NX], zdev[direction]))
+
+    def end_relay0():
+        relay0(met_p, YREC + 31)
+        sibling(met)
 
     def ring0(i):
         def run():
@@ -195,7 +208,8 @@
 
         return run
 
-    todo0 = [begin0, ring0(1), ring0(3), ring0(2), relay0, step0(1, 0), ring0(5), ring0(7), ring0(6)]
+    todo0 = [lambda: begin0(own_w, YREC), end_begin0, lambda: relay0(met_w, YREC)]
+    todo0 += [ring0(1), ring0(3), ring0(2), end_relay0, step0(1, 0), ring0(5), ring0(7), ring0(6)]
     order = (1, 3, 2, 4, 5, 7, 6)
     todo0 += [step0(1, i) for i in order]
     todo0 += [step0(2, i) for i in (0,) + order] + [step0(3, i) for i in (0,) + order]
@@ -230,8 +244,8 @@
 
         return make
 
-    def begin1():
-        go(lambda: copy(own, own, ringsend, wr.at[32], ydev))
+    def begin1(part):
+        go(lambda: copy(part, part, ringsend, wr.at[32], ydev))
 
     def spread(k):
         go(xmove(0, k))
@@ -271,7 +285,7 @@
 
         return run
 
-    todo1 = [begin1, first1]
+    todo1 = [lambda: begin1(own_w), lambda: begin1(own_p), first1]
     for k in range(1, 8):
         todo1.append(zstep1(k))
         if k >= 3:
@@ -308,6 +322,8 @@
         each(1, NT, send)
         wfull[yl, xa, z, core, :, HIDL:HIDP] = pgt[p_row]
 
+    advance(1, 1)
+
     @pl.when(carries)
     def _():
         def send(d):
@@ -347,7 +363,7 @@
     def _():
         copy(p_src, own_p, ps, pr, tdev[0]).wait_recv()
 
-    advance(1, 1)
+    advance(2, 1)
 
     slot = grp % 2
 
@@ -368,7 +384,9 @@
         each(1, NG, send)
         s2dst[slot] = s2src[grp]
 
-    advance(3, 1)
+    advance(4, 1)
+    for direction in (0, 1):
+        x_move(direction, direction).start()
 
     copy(usend.at[0:3], urecv.at[0:3], us, ur, tdev[0]).wait_recv()
     summed = jnp.sum(urecv[...].astype(F32), axis=0)
@@ -410,9 +428,11 @@
         copy(part, part, ds, dr, {"tp": peer_t(d)}).start()
 
     each(1, NT, send_dz)
-    advance(12, 2)
+    advance(11, 4)
 
     copy(dzfull.at[0:3], dzfull.at[0:3], ds, dr, tdev[0]).wait_recv()
+    for direction in (0, 1):
+        x_move(direction, 1 - direction).start()
     dzall = dzfull[:, :, 0:128].reshape(256, 128)
     tails = dzfull[:, :, 128:256].reshape(256, 128).astype(F32)
     lane = iota((256, 128), 1)
@@ -441,13 +461,11 @@
 
     each(1, NP, send_rs)
     rs_dst[p] = rs_src[p]
-    for direction, h in ((0, 0), (1, 1), (0, 1), (1, 0)):
-        x_move(direction, h).start()
-    advance(8, 9)
+    advance(8, 7)
     for direction in (0, 1):
         x_move(direction, direction).wait_recv()
         x_forward(direction).start()
-    advance(4, 11)
+    advance(4, 5)
 
     copy(rs_src.at[0:15], rs_dst.at[0:15], rss, rsr, near_p).wait_recv()
     part = jnp.sum(rs_dst[...].astype(F32), axis=0)
@@ -459,7 +477,7 @@
         copy(zbuf.at[grp], zbuf.at[grp], zss, zsr, {"fsdp": dev}).start()
 
     each(1, NG, send_z)
-    advance(4, 4)
+    advance(4, 12)
     copy(zbuf.at[0:7], zbuf.at[0:7], zss, zsr, near_g).wait_recv()
     part = jnp.sum(zbuf[...].astype(F32), axis=0)
     ag[p] = part[:, 0:256].astype(BF)

time: 64 us -> 59.3 us (0.927)
  Pallas kernels: 59.3 us -> 54.6 us
    pallas_call x1, Pallas kernels: 59.3 us -> 54.6 us  [shards(): pl.pallas_call(kernel, out_shape=results, in_specs=[anywhere] * 7, out_sp...]
where the time goes in v3:
time: 59.3 us; the launch traced here: 59.1 us
  Pallas kernels  54.6 us (92%)
  local copies, waits for them, and re-layouts  3.89 us (7%)
  between operations  0.65 us (1%)
    pallas_call x1, Pallas kernels, shards(): pl.pallas_call(kernel, out_shape=results, in_specs=[anywhere] * 7, out_sp...  54.6 us
    unnamed x10, local copies, waits for them, and re-layouts  3.89 us

profile of v3, /device:TPU:1, one launch (start us, length us, event | category | flops | bytes accessed | tf_op | source)
XLA Modules:
  0.0 59.1 jit_solution(382184459431244649)
XLA Ops:
  0.6 54.6 %shard_map.102 = (bf16[256,1408]{1,0:T(8,128)(2,1)}, f32[128,512]{1,0:T(8,128)}, f32[1,512]{1,0:T(1,128)}, f32[1,128]{1,0:T(1,128)}) custom-call(f32[256,128]{1,0:T(8,128)} %tg_hbm.1, bf16[2,128,512]{2,1,0:T(8,128)(2,1)} %bitcast.6, f32[128,512]{1,0:T(8,128)} %p_hbm.1, f32[1,128]{1,0:T(1,128)} %bitcast.10, f32[1,512]{1,0:T(1,128)} %bitcast.8, ...), custom_call_target="tpu_custom_call" | custom-call | tf_op jit(solution)/shard_map/pallas_call | solution.py:569
  55.2 0.0 copy-start
  55.2 2.1 %copy.15 = bf16[256,1408]{1,0:T(8,128)(2,1)} copy(bf16[256,1408]{1,0:T(8,128)(2,1)} %get-tuple-element.16) | data formatting | bytes 1441792
  57.3 0.0 copy-done
  57.3 0.0 copy-start.1
  57.3 0.7 %copy.16 = f32[128,512]{1,0:T(8,128)} copy(f32[128,512]{1,0:T(8,128)S(1)} %copy-done) | data formatting | bytes 524288
  58.0 0.0 copy-done.1
  58.0 0.0 copy-start.2
  58.0 0.6 copy.17
  58.6 0.0 copy-done.2
  58.6 0.5 copy.18
Async XLA Ops:
  55.2 2.1 %copy-start = (f32[128,512]{1,0:T(8,128)S(1)}, f32[128,512]{1,0:T(8,128)}, u32[]{:S(2)}) copy-start(f32[128,512]{1,0:T(8,128)} %get-tuple-element.17) | copy-start | bytes 786436
  57.3 0.7 %copy-start.1 = (f32[1,512]{1,0:T(1,128)S(1)}, f32[1,512]{1,0:T(1,128)}, u32[]{:S(2)}) copy-start(f32[1,512]{1,0:T(1,128)} %get-tuple-element.10) | copy-start | bytes 6148
  58.0 0.6 %copy-start.2 = (f32[1,128]{1,0:T(1,128)S(1)}, f32[1,128]{1,0:T(1,128)}, u32[]{:S(2)}) copy-start(f32[1,128]{1,0:T(1,128)} %get-tuple-element.11) | copy-start | bytes 1540

commit v4 on v3

--- a/solution.py
+++ b/solution.py
@@ -322,8 +322,6 @@
         each(1, NT, send)
         wfull[yl, xa, z, core, :, HIDL:HIDP] = pgt[p_row]
 
-    advance(1, 1)
-
     @pl.when(carries)
     def _():
         def send(d):
@@ -332,6 +330,8 @@
 
         each(1, NP, send)
         s1dst[p] = s1src[p]
+
+    advance(1, 1)
 
     xv = xfull[t].reshape(256, 512)
     pu = lax.dot_general(xv, pg_hi, NT_DIMS, preferred_element_type=F32)
@@ -385,8 +385,6 @@
         s2dst[slot] = s2src[grp]
 
     advance(4, 1)
-    for direction in (0, 1):
-        x_move(direction, direction).start()
 
     copy(usend.at[0:3], urecv.at[0:3], us, ur, tdev[0]).wait_recv()
     summed = jnp.sum(urecv[...].astype(F32), axis=0)
@@ -428,7 +426,9 @@
         copy(part, part, ds, dr, {"tp": peer_t(d)}).start()
 
     each(1, NT, send_dz)
-    advance(11, 4)
+    for direction in (0, 1):
+        x_move(direction, direction).start()
+    advance(8, 3)
 
     copy(dzfull.at[0:3], dzfull.at[0:3], ds, dr, tdev[0]).wait_recv()
     for direction in (0, 1):
@@ -461,11 +461,7 @@
 
     each(1, NP, send_rs)
     rs_dst[p] = rs_src[p]
-    advance(8, 7)
-    for direction in (0, 1):
-        x_move(direction, direction).wait_recv()
-        x_forward(direction).start()
-    advance(4, 5)
+    advance(10, 9)
 
     copy(rs_src.at[0:15], rs_dst.at[0:15], rss, rsr, near_p).wait_recv()
     part = jnp.sum(rs_dst[...].astype(F32), axis=0)
@@ -477,7 +473,10 @@
         copy(zbuf.at[grp], zbuf.at[grp], zss, zsr, {"fsdp": dev}).start()
 
     each(1, NG, send_z)
-    advance(4, 12)
+    for direction in (0, 1):
+        x_move(direction, direction).wait_recv()
+        x_forward(direction).start()
+    advance(9, 13)
     copy(zbuf.at[0:7], zbuf.at[0:7], zss, zsr, near_g).wait_recv()
     part = jnp.sum(zbuf[...].astype(F32), axis=0)
     ag[p] = part[:, 0:256].astype(BF)

time: 59.3 us -> 57.9 us (0.976)
  Pallas kernels: 54.6 us -> 52.9 us
    pallas_call x1, Pallas kernels: 54.6 us -> 52.9 us  [shards(): pl.pallas_call(kernel, out_shape=results, in_specs=[anywhere] * 7, out_sp...]
where the time goes in v4:
time: 57.9 us; the launch traced here: 57.4 us
  Pallas kernels  52.9 us (91%)
  local copies, waits for them, and re-layouts  3.89 us (7%)
  between operations  0.65 us (1%)
    pallas_call x1, Pallas kernels, shards(): pl.pallas_call(kernel, out_shape=results, in_specs=[anywhere] * 7, out_sp...  52.9 us
    unnamed x10, local copies, waits for them, and re-layouts  3.89 us

profile of v4, /device:TPU:1, one launch (start us, length us, event | category | flops | bytes accessed | tf_op | source)
XLA Modules:
  0.0 57.4 jit_solution(6752944059000139870)
XLA Ops:
  0.6 52.9 %shard_map.102 = (bf16[256,1408]{1,0:T(8,128)(2,1)}, f32[128,512]{1,0:T(8,128)}, f32[1,512]{1,0:T(1,128)}, f32[1,128]{1,0:T(1,128)}) custom-call(f32[256,128]{1,0:T(8,128)} %tg_hbm.1, bf16[2,128,512]{2,1,0:T(8,128)(2,1)} %bitcast.6, f32[128,512]{1,0:T(8,128)} %p_hbm.1, f32[1,128]{1,0:T(1,128)} %bitcast.10, f32[1,512]{1,0:T(1,128)} %bitcast.8, ...), custom_call_target="tpu_custom_call" | custom-call | tf_op jit(solution)/shard_map/pallas_call | solution.py:568
  53.5 0.0 copy-start
  53.5 2.1 %copy.15 = bf16[256,1408]{1,0:T(8,128)(2,1)} copy(bf16[256,1408]{1,0:T(8,128)(2,1)} %get-tuple-element.16) | data formatting | bytes 1441792
  55.6 0.0 copy-done
  55.6 0.0 copy-start.1
  55.6 0.7 %copy.16 = f32[128,512]{1,0:T(8,128)} copy(f32[128,512]{1,0:T(8,128)S(1)} %copy-done) | data formatting | bytes 524288
  56.3 0.0 copy-done.1
  56.3 0.0 copy-start.2
  56.3 0.6 %copy.17 = f32[512]{0:T(512)} copy(f32[512]{0:T(512)S(1)} %bitcast.9) | data formatting | bytes 4096
  56.9 0.0 copy-done.2
  56.9 0.5 copy.18
Async XLA Ops:
  53.5 2.1 %copy-start = (f32[128,512]{1,0:T(8,128)S(1)}, f32[128,512]{1,0:T(8,128)}, u32[]{:S(2)}) copy-start(f32[128,512]{1,0:T(8,128)} %get-tuple-element.17) | copy-start | bytes 786436
  55.6 0.7 %copy-start.1 = (f32[1,512]{1,0:T(1,128)S(1)}, f32[1,512]{1,0:T(1,128)}, u32[]{:S(2)}) copy-start(f32[1,512]{1,0:T(1,128)} %get-tuple-element.10) | copy-start | bytes 6148
  56.3 0.6 %copy-start.2 = (f32[1,128]{1,0:T(1,128)S(1)}, f32[1,128]{1,0:T(1,128)}, u32[]{:S(2)}) copy-start(f32[1,128]{1,0:T(1,128)} %get-tuple-element.11) | copy-start | bytes 1540

commit v5 on v4

--- a/solution.py
+++ b/solution.py
@@ -72,11 +72,20 @@
         )
 
     def each(lo, hi, body):
-        def step(d, carry):
+        for d in range(lo, hi):
             body(d)
-            return carry
-
-        lax.fori_loop(lo, hi, step, 0)
+
+    near_p = {"fsdp": peer_p(1)[1]}
+    near_g = {"fsdp": peer_g(1)[1]}
+
+    bar = pltpu.get_barrier_semaphore()
+
+    def greet(dev):
+        pl.semaphore_signal(bar, inc=1, device_id=dev, device_id_type=MESH)
+
+    each(1, NP, lambda d: greet({"fsdp": peer_p(d)[1]}))
+    each(1, NG, lambda d: greet({"fsdp": peer_g(d)[1]}))
+    each(1, NT, lambda d: greet({"tp": peer_t(d)}))
 
     loads = [
         pltpu.make_async_copy(src, dst, ins.at[i])
@@ -87,18 +96,6 @@
     ]
     for load in loads:
         load.start()
-
-    near_p = {"fsdp": peer_p(1)[1]}
-    near_g = {"fsdp": peer_g(1)[1]}
-
-    bar = pltpu.get_barrier_semaphore()
-
-    def greet(dev):
-        pl.semaphore_signal(bar, inc=1, device_id=dev, device_id_type=MESH)
-
-    each(1, NP, lambda d: greet({"fsdp": peer_p(d)[1]}))
-    each(1, NG, lambda d: greet({"fsdp": peer_g(d)[1]}))
-    each(1, NT, lambda d: greet({"tp": peer_t(d)}))
 
     loads[0].wait()
     wfull[yl, xa, z, core, :, 0:HIDL] = w_ref[...].astype(BF)
@@ -170,7 +167,7 @@
             go(lambda: copy(part, part, ringsend, wr.at[direction * 32], zdev[direction]))
 
     def end_begin0():
-        begin0(own_p, YREC + 31)
+        begin0(own_p, YREC - 1)
         sibling(own)
 
     def relay0(part, yrec):
@@ -181,7 +178,7 @@
             go(lambda: copy(part, part, ringsend, wr.at[direction * 32 + NX], zdev[direction]))
 
     def end_relay0():
-        relay0(met_p, YREC + 31)
+        relay0(met_p, YREC - 1)
         sibling(met)
 
     def ring0(i):
@@ -193,18 +190,16 @@
 
     def arrive0(s, direction, i):
         zmove0(direction, s - 1, i)().wait_recv()
-        if s < 3 or (s == 3 and (i < NX) == (direction == 0)):
+        if s < 3 or (s == 3 and (i < 3) == (direction == 0)):
             go(zmove0(direction, s, i))
         sibling(piece0(i, zslot(direction, s)))
 
     def step0(s, i):
         def run():
-            if s < 4 or i < NX:
+            if s < 4 or i < 3:
                 arrive0(s, 0, i)
-            if s < 4:
+            if s < 4 or i >= 3:
                 arrive0(s, 1, i)
-            elif i < NX:
-                arrive0(s, 1, i + NX)
 
         return run
 
@@ -213,7 +208,7 @@
     order = (1, 3, 2, 4, 5, 7, 6)
     todo0 += [step0(1, i) for i in order]
     todo0 += [step0(2, i) for i in (0,) + order] + [step0(3, i) for i in (0,) + order]
-    todo0 += [step0(4, i) for i in (0, 1, 3, 2)]
+    todo0 += [step0(4, i) for i in (0,) + order]
 
     hops = [(0, 0), (0, 1), (1, 1), (0, 2), (1, 2), (0, 3), (1, 3), (0, 4)]
 

time: 57.9 us -> 57.5 us (level)
  no operation moved by 1% of the time
where the time goes in v5:
time: 57.5 us; the launch traced here: 57.3 us
  Pallas kernels  52.8 us (92%)
  local copies, waits for them, and re-layouts  3.89 us (7%)
  between operations  0.65 us (1%)
    pallas_call x1, Pallas kernels, shards(): pl.pallas_call(kernel, out_shape=results, in_specs=[anywhere] * 7, out_sp...  52.8 us
    unnamed x10, local copies, waits for them, and re-layouts  3.89 us

profile of v5, /device:TPU:1, one launch (start us, length us, event | category | flops | bytes accessed | tf_op | source)
XLA Modules:
  0.0 57.3 jit_solution(14473717201424906468)
XLA Ops:
  0.6 52.8 %shard_map.102 = (bf16[256,1408]{1,0:T(8,128)(2,1)}, f32[128,512]{1,0:T(8,128)}, f32[1,512]{1,0:T(1,128)}, f32[1,128]{1,0:T(1,128)}) custom-call(f32[256,128]{1,0:T(8,128)} %tg_hbm.1, bf16[2,128,512]{2,1,0:T(8,128)(2,1)} %bitcast.6, f32[128,512]{1,0:T(8,128)} %p_hbm.1, f32[1,128]{1,0:T(1,128)} %bitcast.10, f32[1,512]{1,0:T(1,128)} %bitcast.8, ...), custom_call_target="tpu_custom_call" | custom-call | tf_op jit(solution)/shard_map/pallas_call | solution.py:563
  53.4 0.0 copy-start
  53.4 2.1 %copy.15 = bf16[256,1408]{1,0:T(8,128)(2,1)} copy(bf16[256,1408]{1,0:T(8,128)(2,1)} %get-tuple-element.16) | data formatting | bytes 1441792
  55.5 0.0 copy-done
  55.5 0.0 copy-start.1
  55.5 0.7 %copy.16 = f32[128,512]{1,0:T(8,128)} copy(f32[128,512]{1,0:T(8,128)S(1)} %copy-done) | data formatting | bytes 524288
  56.2 0.0 copy-done.1
  56.2 0.0 copy-start.2
  56.2 0.6 %copy.17 = f32[512]{0:T(512)} copy(f32[512]{0:T(512)S(1)} %bitcast.9) | data formatting | bytes 4096
  56.8 0.0 copy-done.2
  56.8 0.5 copy.18
Async XLA Ops:
  53.4 2.1 %copy-start = (f32[128,512]{1,0:T(8,128)S(1)}, f32[128,512]{1,0:T(8,128)}, u32[]{:S(2)}) copy-start(f32[128,512]{1,0:T(8,128)} %get-tuple-element.17) | copy-start | bytes 786436
  55.5 0.7 %copy-start.1 = (f32[1,512]{1,0:T(1,128)S(1)}, f32[1,512]{1,0:T(1,128)}, u32[]{:S(2)}) copy-start(f32[1,512]{1,0:T(1,128)} %get-tuple-element.10) | copy-start | bytes 6148
  56.2 0.6 %copy-start.2 = (f32[1,128]{1,0:T(1,128)S(1)}, f32[1,128]{1,0:T(1,128)}, u32[]{:S(2)}) copy-start(f32[1,128]{1,0:T(1,128)} %get-tuple-element.11) | copy-start | bytes 1540
